TPU v7x, 256 devices: a whole 4x4x8 slice. The times are simulated.
256 devices in a mesh: dp: 16 (over y, x), ctx: 16 (over z, core).
Axes of the slice: x: 4, y: 4, z: 8, core: 2. Of those that a mesh axis runs over, the one named last changes fastest.
Arguments:
- frames: bfloat16 [8192, 6144], P('ctx'), may hold values from -6 to 6
- proj_weight: bfloat16 [3, 6144, 4096], P(None, 'ctx', 'dp'), may hold values from -0.078125 to 0.078125
- out_weight: bfloat16 [6144, 4096], P('dp', 'ctx'), may hold values from -0.09375 to 0.09375
- query_gain: float32 [4096], P('dp'), may hold values from 0.5 to 2
- key_gain: float32 [4096], P('dp'), may hold values from 0.5 to 2
- key_tiles: int32 [32, 128, 18], P('dp', 'ctx'), may hold values from 0 to 127, as said below
- key_counts: int32 [32, 128], P('dp', 'ctx'), may hold values from 1 to 18
Outputs:
- mixed: bfloat16 [8192, 6144], P('ctx', 'dp')
Inputs may be any that keep to these rules, and one draw needn't show every extreme that they name: `key_tiles`: tiles have coordinates (frame layer, height, width) on a grid of 16 x 2 x 4, tile number (layer * 2 + height) * 4 + width. For each head and query tile, the first key_counts entries are distinct tiles that differ from the query tile by at most one in each coordinate, the query tile itself among them; the other entries repeat the query tile. In every head some tile lists its whole window.
All inputs are finite; a program needn't handle non-finite values.
Results may differ from a plain program's by a relative error of at most 0.0088.
Values may be sent and summed in bfloat16 or wider, within the bound.
A program may use at most 64 MiB of HBM per device.

v0:
```python
import jax
import jax.numpy as jnp
from jax import lax
from jax.sharding import PartitionSpec as P

TILE = 64


eps = 1e-06


def padded(block, sides, width):
    for axis, dim in sides:
        count = lax.axis_size(axis)
        forward = [(i, i + 1) for i in range(count - 1)]
        backward = [(target, source) for source, target in forward]
        low = lax.ppermute(
            lax.slice_in_dim(block, block.shape[dim] - width, None, axis=dim), axis, forward
        )
        high = lax.ppermute(lax.slice_in_dim(block, 0, width, axis=dim), axis, backward)
        block = jnp.concatenate([low, block, high], axis=dim)
    return block


def normed(rows, gain):
    stat = jnp.mean(rows * rows, axis=-1, keepdims=True)
    return rows * lax.rsqrt(stat + eps) * gain


def attend(query_rows, key_rows, value_rows, tile_ids, tile_counts, first_tile):
    heads = tile_ids.shape[0]
    slots = tile_ids.shape[2]
    head_dim = query_rows.shape[1] // heads
    query_tiles = query_rows.reshape(-1, TILE, heads, head_dim).transpose(2, 0, 1, 3)
    key_tiles = key_rows.reshape(-1, TILE, heads, head_dim).transpose(2, 0, 1, 3)
    value_tiles = value_rows.reshape(-1, TILE, heads, head_dim).transpose(2, 0, 1, 3)
    local_ids = tile_ids - first_tile
    picked_keys = jax.vmap(lambda lookup, indices: lookup[indices])(key_tiles, local_ids)
    picked_values = jax.vmap(lambda lookup, indices: lookup[indices])(value_tiles, local_ids)
    count_q = query_tiles.shape[1]
    picked_keys = picked_keys.reshape(heads, count_q, slots * TILE, head_dim)
    picked_values = picked_values.reshape(heads, count_q, slots * TILE, head_dim)
    scores = jnp.einsum(
        "hqtd,hqsd->hqts", query_tiles, picked_keys, preferred_element_type=jnp.float32
    ) * head_dim ** (-0.5)
    live = (jnp.arange(slots, dtype=jnp.int32)[None, None, :] < tile_counts[:, :, None]).astype(
        jnp.float32
    )
    live = jnp.repeat(live, TILE, axis=2)[:, :, None, :]
    weights = jnp.exp(scores) * live
    totals = jnp.sum(weights, axis=-1, keepdims=True)
    summed = (
        jnp.einsum(
            "hqts,hqsd->hqtd",
            weights.astype(jnp.bfloat16),
            picked_values,
            preferred_element_type=jnp.float32,
        )
        / totals
    )
    return summed.astype(jnp.bfloat16).transpose(1, 2, 0, 3).reshape(-1, heads * head_dim)


def body(frames, proj_weight, out_weight, query_gain, key_gain, key_tiles, key_counts):
    heads = key_tiles.shape[0]
    width = proj_weight.shape[2]
    head_dim = width // heads
    layer_tiles = key_tiles.shape[1]
    tok_count = frames.shape[0]
    columns = frames
    proj = jnp.einsum(
        "tn,cnw->ctw",
        columns,
        lax.all_gather(proj_weight, "ctx", axis=1, tiled=True),
        preferred_element_type=jnp.float32,
    )
    query_rows = normed(proj[0].reshape(-1, heads, head_dim), query_gain.reshape(heads, head_dim))
    key_rows = normed(proj[1].reshape(-1, heads, head_dim), key_gain.reshape(heads, head_dim))
    query_rows = query_rows.reshape(-1, width).astype(jnp.bfloat16)
    key_rows = key_rows.reshape(-1, width).astype(jnp.bfloat16)
    value_rows = proj[2].astype(jnp.bfloat16)
    paired = jnp.stack([key_rows, value_rows], axis=0)
    widened = padded(paired, (("ctx", 1),), tok_count)
    first_tile = (lax.axis_index("ctx") - 1) * layer_tiles
    attended = attend(query_rows, widened[0], widened[1], key_tiles, key_counts, first_tile)
    out_columns = lax.all_gather(out_weight, "ctx", axis=1, tiled=True)
    columns = out_columns
    mixed = lax.dot_general(
        lax.all_gather(attended, "dp", axis=1, tiled=True),
        columns,
        (((1,), (1,)), ((), ())),
        preferred_element_type=jnp.float32,
    )
    return mixed.astype(jnp.bfloat16)


def solution(mesh):
    placed = (
        P("ctx", None),
        P(None, "ctx", "dp"),
        P("dp", "ctx"),
        P("dp"),
        P("dp"),
        P("dp", "ctx", None),
        P("dp", "ctx"),
    )
    return jax.shard_map(
        body, mesh=mesh, in_specs=placed, out_specs=P("ctx", "dp"), check_vma=False
    )
```

profile of v0, /device:TPU:1, one launch (start us, length us, event | category | flops | bytes accessed | tf_op | source)
XLA Modules:
  0.0 201.2 jit_solution(7556137137856312792)
XLA Ops:
  6.5 0.0 all-gather.4.cloned.1.call-start
  6.5 2.1 %copy.12 = bf16[3,384,256]{1,2,0:T(8,128)(2,1)} copy(bf16[3,384,256]{2,1,0:T(8,128)(2,1)} %param.8) | data formatting | bytes 1179648 | tf_op args[1]
  8.7 0.0 all-gather.4.cloned.1.call-update
  8.7 0.0 all-gather.8.cloned.1.call-start
  8.8 0.7 all-gather.8.cloned.1.call-update
  9.5 0.0 all-gather.6.cloned.1.call-start
  9.5 0.7 fusion.23
  10.2 0.0 copy-start.1
  10.2 64.0 %all-gather.4.cloned.1.call-done = bf16[3,6144,256]{1,2,0:T(8,128)(2,1)} async-done(((bf16[3,384,256]{1,2,0:T(8,128)(2,1)}), bf16[3,6144,256]{1,2,0:T(8,128)(2,1)}) %all-gather.4.cloned.1.call-update) | async-done | bytes 9437200 | tf_op jit(solution)/shard_map/all_gather | solution.py:74
  74.2 9.5 %fusion.4 = f32[3,512,256]{1,2,0:T(8,128)S(1)} fusion(bf16[3,6144,256]{1,2,0:T(8,128)(2,1)} %all-gather.4.cloned.1.call-done, bf16[512,6144]{1,0:T(8,128)(2,1)} %param.7), kind=kOutput, calls=%fused_computation.9 | convolution fusion | flops 4831838208 | bytes 17301504 | tf_op jit(solution)/shard_map/tn,cnw->ctw/dot_general | solution.py:71
  83.7 0.0 copy-start.3
  83.8 0.0 copy-start.2
  83.8 0.1 reduce_sum.28
  83.9 0.0 copy-done.1
  83.9 0.2 slice_multiply_fusion.1
  84.1 0.1 pad_maximum_fusion.1
  84.2 1.9 collective-permute-start
  86.1 3.4 %collective-permute-start.1 = (bf16[2,512,256]{1,2,0:T(8,128)(2,1)S(1)}, bf16[2,512,256]{1,2,0:T(8,128)(2,1)}, u32[]{:S(2)}, u32[]{:S(2)}) collective-permute-start(bf16[2,512,256]{1,2,0:T(8,128)(2,1)S(1)} %pad_maximum_fusion.1), channel_id=1, source_target_pairs={{1,0},{2,1},{3,2},{4,3},{5,4},{6,5},{7,6},{8,7},{9,8},{10,9},{11,1... | collective-permute-start | bytes 1572872 | tf_op jit(solution)/shard_map/ppermute | solution.py:20
  89.5 0.0 copy-done.3
  89.5 0.1 fusion.24
  89.5 0.1 reshape.68
  89.6 0.1 broadcast_in_dim.5
  89.7 0.1 mul.100
  89.8 0.2 copy.13
  90.0 0.3 reshape_squeeze.10
  90.3 0.1 reduce_sum.27
  90.4 0.1 copy.14
  90.6 0.0 copy-done.2
  90.6 0.7 fusion.18
  91.3 3.3 %collective-permute-done = bf16[2,512,256]{1,2,0:T(8,128)(2,1)} collective-permute-done((bf16[2,512,256]{1,2,0:T(8,128)(2,1)S(1)}, bf16[2,512,256]{1,2,0:T(8,128)(2,1)}, u32[]{:S(2)}, u32[]{:S(2)}) %collective-permute-start) | collective-permute-done | bytes 524320 | tf_op jit(solution)/shard_map/ppermute | solution.py:17
  94.6 4.4 %collective-permute-done.1 = bf16[2,512,256]{1,2,0:T(8,128)(2,1)} collective-permute-done((bf16[2,512,256]{1,2,0:T(8,128)(2,1)S(1)}, bf16[2,512,256]{1,2,0:T(8,128)(2,1)}, u32[]{:S(2)}, u32[]{:S(2)}) %collective-permute-start.1) | collective-permute-done | bytes 524320 | tf_op jit(solution)/shard_map/ppermute | solution.py:20
  99.0 1.3 pad_maximum_fusion
  100.3 1.0 fusion.25
  101.3 0.9 reshape.88
  102.2 1.0 copy.16
  103.2 2.4 %reshape.89 = bf16[24,64,2,128]{1,0,3,2:T(8,128)(2,1)S(1)} reshape(bf16[1,1536,256]{1,2,0:T(8,128)(2,1)} %get-tuple-element.9) | data formatting | bytes 1572864 | tf_op jit(solution)/shard_map/reshape;squeeze | solution.py:36
  105.6 1.0 copy.19
  106.6 6.4 %gather_fusion = bf16[288,64,128]{2,1,0:T(8,128)(2,1)} fusion(bf16[2,24,64,128]{3,2,1,0:T(8,128)(2,1)S(1)} %bitcast.53, s32[288]{0:T(512)S(1)} %reshape.68), kind=kCustom, calls=%fused_computation | custom fusion | bytes 9439488 | tf_op jit(solution)/shard_map/vmap()/gather | solution.py:38
  113.0 6.3 %gather_fusion.1 = bf16[288,64,128]{2,1,0:T(8,128)(2,1)} fusion(bf16[2,24,64,128]{3,2,1,0:T(8,128)(2,1)S(1)} %bitcast.54, s32[288]{0:T(512)S(1)} %reshape.68), kind=kCustom, calls=%fused_computation.1 | custom fusion | bytes 9439488 | tf_op jit(solution)/shard_map/vmap()/gather | solution.py:39
  119.3 0.0 copy-start
  119.3 4.5 %fusion.26 = (f32[2,8,64]{2,1,0:T(8,128)S(1)}, bf16[2,8,64,1152]{3,2,1,0:T(8,128)(2,1)S(1)}) fusion(f32[2,8,1152]{2,1,0:T(8,128)S(1)} %mul.100, bf16[2,8,1152,128]{3,2,1,0:T(8,128)(2,1)} %bitcast.56, bf16[2,8,64,128]{3,0,2,1:T(2,128)(2,1)S(1)} %fusion.18), kind=kOutput, calls=%fused_computation.35 | convolution fusion | flops 306707456 | bytes 7417856 | tf_op jit(solution)/shard_map/hqtd,hqsd->hqts/dot_general | solution.py:43
  123.8 0.0 copy-done
  123.8 1.1 fusion.13
  124.9 0.3 copy.20
  125.2 0.7 copy.31
  125.9 0.0 all-gather.6.cloned.1.call-update
  126.0 0.0 all-gather.8.cloned.1.call-done
  126.0 62.4 %all-gather.6.cloned.1.call-done = bf16[512,4096]{1,0:T(8,128)(2,1)} async-done(((bf16[512,256]{1,0:T(8,128)(2,1)}), bf16[512,4096]{1,0:T(8,128)(2,1)}) %all-gather.6.cloned.1.call-update) | async-done | bytes 4194320 | tf_op jit(solution)/shard_map/all_gather | solution.py:89
  188.4 6.3 %convolution_convert_fusion = bf16[512,384]{1,0:T(8,128)(2,1)} fusion(bf16[512,4096]{1,0:T(8,128)(2,1)} %all-gather.6.cloned.1.call-done, bf16[384,4096]{1,0:T(8,128)(2,1)} %all-gather.8.cloned.1.call-done), kind=kOutput, calls=%fused_computation.10 | convolution fusion | flops 1610809344 | bytes 7733248 | tf_op jit(solution)/shard_map/dot_general | solution.py:88
  (4 shorter events, 0.1 us)
Async XLA Ops:
  6.5 67.6 %all-gather.4.cloned.1.call-start = ((), (), s32[]{:S(2)}) async-start(), calls=%async_computation | async-start | bytes 10027008 | tf_op jit(solution)/shard_map/all_gather | solution.py:74
  8.7 117.3 %all-gather.8.cloned.1.call-start = ((), (), s32[]{:S(2)}) async-start(), calls=%async_computation.2 | async-start | bytes 3342336 | tf_op jit(solution)/shard_map/all_gather | solution.py:86
  9.5 178.9 %all-gather.6.cloned.1.call-start = ((), (), s32[]{:S(2)}) async-start(), calls=%async_computation.1 | async-start | bytes 4456448 | tf_op jit(solution)/shard_map/all_gather | solution.py:89
  10.2 73.7 %copy-start.1 = (f32[256]{0:T(256)S(1)}, f32[256]{0:T(256)}, u32[]{:S(2)}) copy-start(f32[256]{0:T(256)} %param.11) | copy-start | bytes 3076
  83.7 5.8 %copy-start.3 = (s32[2,8]{1,0:T(2,128)S(1)}, s32[2,8]{1,0:T(2,128)}, u32[]{:S(2)}) copy-start(s32[2,8]{1,0:T(2,128)} %param.13) | copy-start | bytes 196
  83.8 6.8 %copy-start.2 = (f32[256]{0:T(256)S(1)}, f32[256]{0:T(256)}, u32[]{:S(2)}) copy-start(f32[256]{0:T(256)} %param.10) | copy-start | bytes 3076
  84.2 10.4 %collective-permute-start = (bf16[2,512,256]{1,2,0:T(8,128)(2,1)S(1)}, bf16[2,512,256]{1,2,0:T(8,128)(2,1)}, u32[]{:S(2)}, u32[]{:S(2)}) collective-permute-start(bf16[2,512,256]{1,2,0:T(8,128)(2,1)S(1)} %pad_maximum_fusion.1), channel_id=1, source_target_pairs={{0,1},{1,2},{2,3},{3,4},{4,5},{5,6},{6,7},{7,8},{8,9},{9,10},{10,1... | collective-permute-start | bytes 1572872 | tf_op jit(solution)/shard_map/ppermute | solution.py:17
  86.1 12.9 %collective-permute-start.1 = (bf16[2,512,256]{1,2,0:T(8,128)(2,1)S(1)}, bf16[2,512,256]{1,2,0:T(8,128)(2,1)}, u32[]{:S(2)}, u32[]{:S(2)}) collective-permute-start(bf16[2,512,256]{1,2,0:T(8,128)(2,1)S(1)} %pad_maximum_fusion.1), channel_id=1, source_target_pairs={{1,0},{2,1},{3,2},{4,3},{5,4},{6,5},{7,6},{8,7},{9,8},{10,9},{11,1... | collective-permute-start | bytes 1572872 | tf_op jit(solution)/shard_map/ppermute | solution.py:20
  119.3 4.5 %copy-start = (bf16[288,64,128]{2,1,0:T(8,128)(2,1)S(1)}, bf16[288,64,128]{2,1,0:T(8,128)(2,1)}, u32[]{:S(2)}) copy-start(bf16[288,64,128]{2,1,0:T(8,128)(2,1)} %gather_fusion.1) | copy-start | bytes 14155780
Sparse Core Ops, SparseCore 0:
  9.1 64.9 all-gather.3
  75.9 45.6 all-gather.7
  126.1 62.2 all-gather.5
where the time goes:
time: 202 us; the launch traced here: 201 us
  waiting for transfers between devices  135 us (67%)
  local copies, waits for them, and re-layouts  23 us (11%)
  matrix products  21.4 us (11%)
  between operations  13.3 us (7%)
  starting transfers between devices  5.36 us (3%)
  other arithmetic  3.22 us (2%)
    all_gather x1, waiting for transfers between devices, body(): lax.all_gather(proj_weight, 'ctx', axis=1, tiled=True)  64 us
    all_gather x1, waiting for transfers between devices, body(): lax.all_gather(attended, 'dp', axis=1, tiled=True)  62.4 us
    gather x3, local copies, waits for them, and re-layouts, attend(): lookup[indices]  12.7 us
    dot_general x1, matrix products, body(): jnp.einsum('tn,cnw->ctw', columns, lax.all_gather(proj_weight, 'ctx', axi...  9.52 us
    dot_general x1, matrix products, body(): lax.dot_general(lax.all_gather(attended, 'dp', axis=1, tiled=True), colum...  6.26 us
    dot_general x1, matrix products, attend(): jnp.einsum('hqtd,hqsd->hqts', query_tiles, picked_keys, preferred_element...  4.49 us
    ppermute x1, waiting for transfers between devices, padded(): lax.ppermute(lax.slice_in_dim(block, 0, width, axis=dim), axis, backward)  4.43 us
  transfers between devices with their start and end apart: 5, of which 4 were waited for; matrix products, arithmetic and copies ran while one was open for 19% of the time, Pallas kernels for 0%

commit v1 on v0

v1 whole, which is shorter than its diff:
```python
import math

import jax
import jax.numpy as jnp
from jax import lax
from jax.experimental import pallas as pl
from jax.experimental.pallas import tpu as pltpu
from jax.sharding import PartitionSpec as P

MESH = pl.DeviceIdType.MESH
F32, BF16 = jnp.float32, jnp.bfloat16

D = 6144
HD = 128
TILE = 64
TOK = 512
QT = 8
SLOTS = 18
NZ = 8
NX = 4
NY = 4
NC = 16
ROWS = 384
HALF = 192
KEYS = 3 * TOK
EPS = 1e-06
SCALE = math.log2(math.e) / math.sqrt(HD)

ROUNDS = ((1, 0), (2, 0), (0, 0), (1, 1), (2, 1), (0, 1), (3, 0), (3, 1))


def kernel(fr_hbm, pw_hbm, ow_hbm, qg, kg, kt, kc, out, wg, fr, acc, qbuf, kv, att, mask, oacc,
           fsem, osem, zsend, zrecv, bsend, brecv, hsend, hrecv, gsend, grecv):
    dp, c = lax.axis_index("dp"), lax.axis_index("ctx")
    z, core = c // 2, c % 2
    x, y = dp % NX, dp // NX
    sib = (dp, z * 2 + 1 - core)
    prv, nxt = (dp, (c + NC - 1) % NC), (dp, (c + 1) % NC)

    def zdev(step):
        return (dp, ((z + step + NZ) % NZ) * 2 + core)

    def xydev(i, j):
        return (((y + j + NY) % NY) * NX + (x + i + NX) % NX, c)

    frames = pltpu.make_async_copy(fr_hbm, fr, fsem)
    own = []
    for r, (j, h) in enumerate(ROUNDS):
        cols = pl.ds(h * HD, HD)
        src = ow_hbm.at[:, cols] if j == 3 else pw_hbm.at[j, :, cols]
        own.append(pltpu.make_async_copy(src, wg.at[r, c], osem.at[r]))
    for copy in own:
        copy.start()
    frames.start()

    barrier = pltpu.get_barrier_semaphore()
    greeted = [zdev(1), zdev(-1), prv, nxt, xydev(1, 0), xydev(-1, 0), xydev(0, 1), xydev(0, -1)]
    for device in greeted:
        pl.semaphore_signal(barrier, inc=1, device_id=device, device_id_type=MESH)
    pl.semaphore_wait(barrier, len(greeted))

    def zcopy(direction, r, owner, hop, half=False):
        piece = wg.at[r, owner * 2 + core]
        if half:
            piece = piece.at[pl.ds(direction * HALF, HALF)]
        return pltpu.make_async_remote_copy(
            src_ref=piece, dst_ref=piece, send_sem=zsend, recv_sem=zrecv.at[direction, r, hop],
            device_id=zdev(1 - 2 * direction), device_id_type=MESH,
        )

    def bcopy(r, owner, which):
        piece = wg.at[r, owner * 2 + which]
        return pltpu.make_async_remote_copy(
            src_ref=piece, dst_ref=piece, send_sem=bsend, recv_sem=brecv.at[r, owner],
            device_id=sib, device_id_type=MESH,
        )

    def send_own(r):
        zcopy(0, r, z, 0).start()
        zcopy(1, r, z, 0).start()
        bcopy(r, z, core).start()

    def zat(step):
        return (z + step + NZ) % NZ

    for copy in own:
        copy.wait()
    send_own(0)
    send_own(1)

    lane_tile = lax.broadcasted_iota(jnp.int32, (QT, KEYS), 1) // TILE + (c - 1) * QT
    row = lax.broadcasted_iota(jnp.int32, (QT, QT), 0)
    col = lax.broadcasted_iota(jnp.int32, (QT, QT), 1)
    for h in range(2):
        counts = jnp.sum(
            jnp.where(row == col, kc[h:h + 1, :].astype(F32), 0.0), axis=1, keepdims=True
        ).astype(jnp.int32)
        listed = jnp.zeros((QT, KEYS), F32)
        for s in range(SLOTS):
            tile = jnp.where(s < counts, kt[h, :, s:s + 1], -1000)
            listed = jnp.where(lane_tile == tile, 1.0, listed)
        for i in range(QT):
            mask[h, i] = listed[i:i + 1, :]

    frames.wait()

    def project(r, owner, first=False):
        cols = pl.ds(pl.multiple_of(owner * (2 * ROWS), 2 * ROWS), 2 * ROWS)
        weight = wg[r, pl.ds(owner * 2, 2)].reshape(2 * ROWS, HD)
        part = jnp.dot(fr[:, cols], weight, preferred_element_type=F32)
        if first:
            acc[r] = part
        else:
            acc[r] += part

    def normed(r, gain):
        rows = acc[r]
        stat = jnp.mean(rows * rows, axis=-1, keepdims=True)
        return (rows * lax.rsqrt(stat + EPS) * gain).astype(BF16)

    def halo(h, which, side):
        slot = 2 - 2 * side
        return pltpu.make_async_remote_copy(
            src_ref=kv.at[h, which, 1], dst_ref=kv.at[h, which, slot], send_sem=hsend,
            recv_sem=hrecv.at[h, which, side], device_id=(prv, nxt)[side], device_id_type=MESH,
        )

    def send_halo(h, which):
        halo(h, which, 0).start()
        halo(h, which, 1).start()

    def attention(h):
        for which in range(2):
            for side in range(2):
                halo(h, which, side).wait_recv()

        def block(b, carry):
            rows = pl.ds(pl.multiple_of(b * 128, 128), 128)
            keys = kv[h, 0].reshape(KEYS, HD)
            values = kv[h, 1].reshape(KEYS, HD)
            scores = lax.dot_general(
                qbuf[rows, :], keys, (((1,), (1,)), ((), ())), preferred_element_type=F32
            )
            live = jnp.concatenate(
                [jnp.broadcast_to(mask[h, b * 2 + i], (TILE, KEYS)) for i in range(2)], axis=0
            )
            weights = jnp.where(live > 0.5, jnp.exp2(scores * SCALE), 0.0)
            total = jnp.sum(weights, axis=-1, keepdims=True)
            summed = jnp.dot(weights.astype(BF16), values, preferred_element_type=F32)
            att[h, dp, rows, :] = (summed / total).astype(BF16)
            return carry

        lax.fori_loop(0, TOK // 128, block, 0)

    def gcopy(h, part, stage, direction, hop, across, along):
        i, j = (across, along) if part == 0 else (along, across)
        owner = ((y + j + NY) % NY) * NX + (x + i + NX) % NX
        start, size = part * 256, 256
        if hop == 1:
            start, size = start + direction * 128, 128
        piece = att.at[h, owner, pl.ds(start, size)]
        step = 1 - 2 * direction
        on_first = stage == 0
        target = xydev(step, 0) if on_first == (part == 0) else xydev(0, step)
        return pltpu.make_async_remote_copy(
            src_ref=piece, dst_ref=piece, send_sem=gsend,
            recv_sem=grecv.at[h, part, stage, direction, hop], device_id=target, device_id_type=MESH,
        )

    OFF = (0, -1, 1, 2)

    def first_send(h, part, direction, hop):
        gcopy(h, part, 0, direction, hop, 0 if hop == 0 else (-1 if direction == 0 else 1), 0).start()

    def first_wait(h, part, direction, hop):
        away = 2 if hop == 1 else (-1 if direction == 0 else 1)
        gcopy(h, part, 0, direction, hop, away, 0).wait_recv()

    def second_send(h, part, k, direction, hop):
        along = 0 if hop == 0 else (-1 if direction == 0 else 1)
        gcopy(h, part, 1 + k, direction, hop, OFF[k], along).start()

    def second_wait(h, part, k, direction, hop):
        along = 2 if hop == 1 else (-1 if direction == 0 else 1)
        gcopy(h, part, 1 + k, direction, hop, OFF[k], along).wait_recv()

    both = [(part, direction) for part in range(2) for direction in range(2)]

    def gather0(h):
        for part, direction in both:
            first_send(h, part, direction, 0)
        for part, direction in both:
            second_send(h, part, 0, direction, 0)

    def gather1(h):
        for part, direction in both:
            first_wait(h, part, direction, 0)
            first_send(h, part, direction, 1)
            for d in range(2):
                second_send(h, part, 1 + direction, d, 0)
        for part, direction in both:
            second_wait(h, part, 0, direction, 0)
            second_send(h, part, 0, direction, 1)

    def gather2(h):
        for part in range(2):
            for direction in range(2):
                first_wait(h, part, direction, 1)
            for d in range(2):
                second_send(h, part, 3, d, 0)
        for k in (1, 2):
            for part, direction in both:
                second_wait(h, part, k, direction, 0)
                second_send(h, part, k, direction, 1)

    def gather3(h):
        for part, direction in both:
            second_wait(h, part, 3, direction, 0)
            second_send(h, part, 3, direction, 1)
        for k in (0, 1, 2):
            for part, direction in both:
                second_wait(h, part, k, direction, 1)

    def gather4(h):
        for part, direction in both:
            second_wait(h, part, 3, direction, 1)

    def tick(t, carry):
        p, s = t // 4, t % 4 + 1
        for lane in range(2):
            r = 2 * p + lane

            @pl.when(s < 4)
            def _():
                zcopy(0, r, zat(-s), s - 1).wait_recv()

                @pl.when(s < 3)
                def _():
                    zcopy(0, r, zat(-s), s).start()

                @pl.when(s == 3)
                def _():
                    zcopy(0, r, zat(-s), 3, True).start()

                bcopy(r, zat(-s), core).start()
                zcopy(1, r, zat(s), s - 1).wait_recv()

                @pl.when(s < 3)
                def _():
                    zcopy(1, r, zat(s), s).start()

                @pl.when(s == 3)
                def _():
                    zcopy(1, r, zat(s), 3, True).start()

                bcopy(r, zat(s), core).start()

            @pl.when(s == 4)
            def _():
                @pl.when(p < 3)
                def _():
                    send_own(r + 2)

                zcopy(0, r, zat(4), 3, True).wait_recv()
                zcopy(1, r, zat(4), 3, True).wait_recv()
                bcopy(r, zat(4), core).start()

        for step, gather in ((1, gather1), (2, gather2), (3, gather3), (4, gather4)):
            @pl.when((p >= 2) & (s == step))
            def _():
                gather(p - 2)

        for lane in range(2):
            r = 2 * p + lane

            @pl.when(s == 1)
            def _():
                bcopy(r, z, 1 - core).wait_recv()

                @pl.when(p < 3)
                def _():
                    project(r, z, first=True)

            bcopy(r, zat(-s), 1 - core).wait_recv()

            @pl.when(s < 4)
            def _():
                bcopy(r, zat(s), 1 - core).wait_recv()

            @pl.when(p < 3)
            def _():
                project(r, zat(-s))

                @pl.when(s < 4)
                def _():
                    project(r, zat(s))

        @pl.when((s == 4) & (p == 0))
        def _():
            kv[0, 0, 1] = normed(0, kg[0:1, :])
            send_halo(0, 0)
            kv[0, 1, 1] = acc[1].astype(BF16)
            send_halo(0, 1)

        @pl.when((s == 4) & (p == 1))
        def _():
            kv[1, 0, 1] = normed(3, kg[1:2, :])
            send_halo(1, 0)
            qbuf[...] = normed(2, qg[0:1, :])

        @pl.when((s == 4) & (p == 2))
        def _():
            kv[1, 1, 1] = acc[4].astype(BF16)
            send_halo(1, 1)
            qbuf[...] = normed(5, qg[1:2, :])

        @pl.when((s == 4) & (p >= 1) & (p < 3))
        def _():
            attention(p - 1)
            gather0(p - 1)

        return carry

    lax.fori_loop(0, 16, tick, 0)

    oacc[...] = jnp.zeros_like(oacc)

    def mix(i, carry):
        h, d = i // 4, i % 4 * 4
        left = jnp.concatenate([att[h, d + k] for k in range(4)], axis=1)
        right = jnp.concatenate([wg[6 + h, d + k] for k in range(4)], axis=1)
        oacc[...] += lax.dot_general(
            left, right, (((1,), (1,)), ((), ())), preferred_element_type=F32
        )
        return carry

    lax.fori_loop(0, 8, mix, 0)
    out[...] = oacc[...].astype(BF16)

    for sent, sem in (
        (wg.at[pl.ds(0, 7), pl.ds(0, 8)], zsend),
        (wg.at[pl.ds(0, 4)], bsend),
        (kv.at[:, :, pl.ds(0, 2)], hsend),
        (att.at[:, pl.ds(0, 15)], gsend),
    ):
        pltpu.make_async_copy(sent, sent, sem).wait()


def body(frames, proj_weight, out_weight, query_gain, key_gain, key_tiles, key_counts):
    anywhere = pl.BlockSpec(memory_space=pl.ANY)
    vmem = pl.BlockSpec(memory_space=pltpu.VMEM)
    dma = pltpu.SemaphoreType.DMA
    return pl.pallas_call(
        kernel,
        out_shape=jax.ShapeDtypeStruct((TOK, ROWS), BF16),
        in_specs=[anywhere] * 3 + [vmem] * 4,
        out_specs=vmem,
        scratch_shapes=[
            pltpu.VMEM((8, NC, ROWS, HD), BF16),
            pltpu.VMEM((TOK, D), BF16),
            pltpu.VMEM((6, TOK, HD), F32),
            pltpu.VMEM((TOK, HD), BF16),
            pltpu.VMEM((2, 2, 3, TOK, HD), BF16),
            pltpu.VMEM((2, 16, TOK, HD), BF16),
            pltpu.VMEM((2, QT, 1, KEYS), F32),
            pltpu.VMEM((TOK, ROWS), F32),
            dma, dma((8,)),
            dma, dma((2, 8, 4)),
            dma, dma((8, 8)),
            dma, dma((2, 2, 2)),
            dma, dma((2, 2, 5, 2, 2)),
        ],
        compiler_params=pltpu.CompilerParams(
            collective_id=0, has_side_effects=True, vmem_limit_bytes=56 * 2**20
        ),
        cost_estimate=pl.CostEstimate(
            flops=8 * 10**9, bytes_accessed=8 * 10**6, transcendentals=2 * 10**6
        ),
        name="layer",
    )(
        frames, proj_weight, out_weight, query_gain.reshape(2, HD), key_gain.reshape(2, HD),
        key_tiles, key_counts,
    )


def solution(mesh):
    placed = (
        P("ctx", None),
        P(None, "ctx", "dp"),
        P("dp", "ctx"),
        P("dp"),
        P("dp"),
        P("dp", "ctx", None),
        P("dp", "ctx"),
    )
    return jax.shard_map(
        body, mesh=mesh, in_specs=placed, out_specs=P("ctx", "dp"), check_vma=False
    )
```

time: 202 us -> 104 us (0.51)
  waiting for transfers between devices: 135 us -> 0 us
  Pallas kernels: 0 us -> 102 us
  matrix products: 21.4 us -> 0 us
  local copies, waits for them, and re-layouts: 23 us -> 1.78 us
  between operations: 13.3 us -> 0.01 us
  starting transfers between devices: 5.36 us -> 0 us
  other arithmetic: 3.22 us -> 0 us
    all_gather x3 -> x0, waiting for transfers between devices: 126 us -> none  [the longest x1 64 us: body(): lax.all_gather(proj_weight, 'ctx', axis=1, tiled=True)]
    pallas_call x0 -> x1, Pallas kernels: none -> 102 us  [body(): pl.pallas_call(kernel, out_shape=jax.ShapeDtypeStruct((TOK, ROWS), BF16),...]
    dot_general x4 -> x0, matrix products: 21.4 us -> none  [the longest x1 9.52 us: body(): jnp.einsum('tn,cnw->ctw', columns, lax.all_gather(proj_weight, 'ctx', axi...]
    gather x3 -> x0, local copies, waits for them, and re-layouts: 12.7 us -> none  [attend(): lookup[indices]]
    ppermute x2 -> x0, waiting for transfers between devices: 7.74 us -> none  [the longest x1 4.43 us: padded(): lax.ppermute(lax.slice_in_dim(block, 0, width, axis=dim), axis, backward)]
    another operation x5 -> x0, local copies, waits for them, and re-layouts: 5.55 us -> none  [the longest x2 3.38 us: attend(): value_rows.reshape(-1, TILE, heads, head_dim).transpose(2, 0, 1, 3)]
    ppermute x2 -> x0, starting transfers between devices: 5.27 us -> none  [the longest x1 3.35 us: padded(): lax.ppermute(lax.slice_in_dim(block, 0, width, axis=dim), axis, backward)]
  transfers between devices with their start and end apart: 5 -> 0, of which waited for: 4 -> 0; matrix products, arithmetic and copies ran while one was open for 19% -> 0% of each run, Pallas kernels for 0% -> 0%
where the time goes in v1:
time: 104 us
  Pallas kernels  102 us (98%)
  local copies, waits for them, and re-layouts  1.78 us (2%)
    pallas_call x1, Pallas kernels, body(): pl.pallas_call(kernel, out_shape=jax.ShapeDtypeStruct((TOK, ROWS), BF16),...  102 us

profile of v1, /device:TPU:1, one launch (start us, length us, event | category | flops | bytes accessed | tf_op | source)
XLA Modules:
  0.0 104.1 jit_solution(7550184349781815671)
XLA Ops:
  0.0 102.3 %layer.1 = bf16[512,384]{1,0:T(8,128)(2,1)} custom-call(bf16[512,6144]{1,0:T(8,128)(2,1)} %fr_hbm.1, bf16[3,384,256]{2,1,0:T(8,128)(2,1)} %pw_hbm.1, bf16[384,256]{1,0:T(8,128)(2,1)} %ow_hbm.1, f32[2,128]{1,0:T(2,128)} %bitcast.2, f32[2,128]{1,0:T(2,128)} %bitcast.3, s32[2,8,18]{2,1,0:T(8,128)} %kt.1, s32[2,8]{1,0:T(2,128)} %kc.1), custom_call_target="tpu_custom_call" | custom-call | flops 8000000000 | bytes 8000000 | tf_op jit(solution)/shard_map/layer/pallas_call | solution.py:353
  102.3 1.8 %copy.9 = bf16[512,384]{1,0:T(8,128)(2,1)} copy(bf16[512,384]{1,0:T(8,128)(2,1)} %layer.1) | data formatting | bytes 786432

commit v2 on v1

v2 whole, which is shorter than its diff:
```python
import math

import jax
import jax.numpy as jnp
from jax import lax
from jax.experimental import pallas as pl
from jax.experimental.pallas import tpu as pltpu
from jax.sharding import PartitionSpec as P

MESH = pl.DeviceIdType.MESH
F32, BF16 = jnp.float32, jnp.bfloat16

D = 6144
HD = 128
TILE = 64
TOK = 512
QT = 8
SLOTS = 18
NZ = 8
NX = 4
NY = 4
NC = 16
ROWS = 384
HALF = 192
KEYS = 3 * TOK
EPS = 1e-06
SCALE = math.log2(math.e) / math.sqrt(HD)

ROUNDS = ((1, 0), (2, 0), (0, 0), (1, 1), (2, 1), (0, 1), (3, 0), (3, 1))


def kernel(fr_hbm, pw_hbm, ow_hbm, qg, kg, kt, kc, out, wg, fr, acc, qbuf, kv, att, mask, oacc, part_sum, part_lanes,
           fsem, osem, zsend, zrecv, bsend, brecv, hsend, hrecv, gsend, grecv):
    dp, c = lax.axis_index("dp"), lax.axis_index("ctx")
    z, core = c // 2, c % 2
    x, y = dp % NX, dp // NX
    sib = (dp, z * 2 + 1 - core)
    prv, nxt = (dp, (c + NC - 1) % NC), (dp, (c + 1) % NC)

    def zdev(step):
        return (dp, ((z + step + NZ) % NZ) * 2 + core)

    def xydev(i, j):
        return (((y + j + NY) % NY) * NX + (x + i + NX) % NX, c)

    frames = pltpu.make_async_copy(fr_hbm, fr, fsem)
    own = []
    for r, (j, h) in enumerate(ROUNDS):
        cols = pl.ds(h * HD, HD)
        src = ow_hbm.at[:, cols] if j == 3 else pw_hbm.at[j, :, cols]
        own.append(pltpu.make_async_copy(src, wg.at[r, c], osem.at[r]))
    for copy in own:
        copy.start()
    frames.start()

    barrier = pltpu.get_barrier_semaphore()
    greeted = [zdev(1), zdev(-1), prv, nxt]
    greeted += [xydev(i, 0) for i in (-1, 1, 2)] + [xydev(0, j) for j in (-1, 1, 2)]
    for device in greeted:
        pl.semaphore_signal(barrier, inc=1, device_id=device, device_id_type=MESH)
    pl.semaphore_wait(barrier, len(greeted))

    def zcopy(direction, r, owner, hop, half=False):
        piece = wg.at[r, owner * 2 + core]
        if half:
            piece = piece.at[pl.ds(direction * HALF, HALF)]
        return pltpu.make_async_remote_copy(
            src_ref=piece, dst_ref=piece, send_sem=zsend, recv_sem=zrecv.at[direction, r, hop],
            device_id=zdev(1 - 2 * direction), device_id_type=MESH,
        )

    def bcopy(r, owner, which):
        piece = wg.at[r, owner * 2 + which]
        return pltpu.make_async_remote_copy(
            src_ref=piece, dst_ref=piece, send_sem=bsend, recv_sem=brecv.at[r, owner],
            device_id=sib, device_id_type=MESH,
        )

    def send_own(r):
        zcopy(0, r, z, 0).start()
        zcopy(1, r, z, 0).start()
        bcopy(r, z, core).start()

    def zat(step):
        return (z + step + NZ) % NZ

    for copy in own:
        copy.wait()
    for r in range(3):
        send_own(r)

    lane_tile = lax.broadcasted_iota(jnp.int32, (QT, KEYS), 1) // TILE + (c - 1) * QT
    row = lax.broadcasted_iota(jnp.int32, (QT, QT), 0)
    col = lax.broadcasted_iota(jnp.int32, (QT, QT), 1)
    for h in range(2):
        counts = jnp.sum(
            jnp.where(row == col, kc[h:h + 1, :].astype(F32), 0.0), axis=1, keepdims=True
        ).astype(jnp.int32)
        listed = jnp.zeros((QT, KEYS), F32)
        for s in range(SLOTS):
            tile = jnp.where(s < counts, kt[h, :, s:s + 1], -1000)
            listed = jnp.where(lane_tile == tile, 1.0, listed)
        for i in range(QT):
            for slot in range(3):
                mask[h, slot, i] = listed[i:i + 1, slot * TOK:(slot + 1) * TOK]

    def project(r, owner, first=False):
        cols = pl.ds(pl.multiple_of(owner * (2 * ROWS), 2 * ROWS), 2 * ROWS)
        weight = wg[r, pl.ds(owner * 2, 2)].reshape(2 * ROWS, HD)
        part = jnp.dot(fr[:, cols], weight, preferred_element_type=F32)
        if first:
            acc[r] = part
        else:
            acc[r] += part

    def normed(r, gain):
        rows = acc[r]
        stat = jnp.mean(rows * rows, axis=-1, keepdims=True)
        return (rows * lax.rsqrt(stat + EPS) * gain).astype(BF16)

    def halo(h, which, side):
        return pltpu.make_async_remote_copy(
            src_ref=kv.at[h, which, 1], dst_ref=kv.at[h, which, 2 - 2 * side], send_sem=hsend,
            recv_sem=hrecv.at[h, which, side], device_id=(dp, (c + NC - 1 + 2 * side) % NC),
            device_id_type=MESH,
        )

    def send_halo(h, which):
        halo(h, which, 1 - core).start()
        halo(h, which, core).start()

    def weigh(h, b, slot):
        rows = pl.ds(pl.multiple_of(b * 128, 128), 128)
        scores = lax.dot_general(
            qbuf[rows, :], kv[h, 0, slot], (((1,), (1,)), ((), ())), preferred_element_type=F32
        )
        live = jnp.concatenate(
            [jnp.broadcast_to(mask[h, slot, b * 2 + i], (TILE, TOK)) for i in range(2)], axis=0
        )
        weights = jnp.where(live > 0.5, jnp.exp2(scores * SCALE), 0.0)
        lanes = sum(weights[:, i * HD:(i + 1) * HD] for i in range(TOK // HD))
        summed = jnp.dot(weights.astype(BF16), kv[h, 1, slot], preferred_element_type=F32)
        return summed, lanes

    def attend_near(h):
        for which in range(2):
            halo(h, which, core).wait_recv()

        def near(b, carry):
            rows = pl.ds(pl.multiple_of(b * 128, 128), 128)
            summed, lanes = weigh(h, b, 1)
            more, more_lanes = weigh(h, b, 2 - 2 * core)
            part_sum[rows, :] = summed + more
            part_lanes[rows, :] = lanes + more_lanes
            return carry

        lax.fori_loop(0, TOK // 128, near, 0)

    def attend_far(h, part):
        if part == 0:
            for which in range(2):
                halo(h, which, 1 - core).wait_recv()

        def far(b, carry):
            rows = pl.ds(pl.multiple_of(b * 128, 128), 128)
            summed, lanes = weigh(h, b, 2 * core)
            total = jnp.sum(part_lanes[rows, :] + lanes, axis=-1, keepdims=True)
            att[h, dp, rows, :] = ((part_sum[rows, :] + summed) / total).astype(BF16)
            return carry

        lax.fori_loop(2 * part, 2 * part + 2, far, 0)
        gather0(h, part)

    def gcopy(h, part, stage, direction, hop, across, along, half, step):
        i, j = (across, along) if part == 0 else (along, across)
        owner = ((y + j + NY) % NY) * NX + (x + i + NX) % NX
        start, size = part * 256, 256
        if half:
            start, size = start + direction * 128, 128
        piece = att.at[h, owner, pl.ds(start, size)]
        target = xydev(step, 0) if (stage == 0) == (part == 0) else xydev(0, step)
        return pltpu.make_async_remote_copy(
            src_ref=piece, dst_ref=piece, send_sem=gsend,
            recv_sem=grecv.at[h, part, stage, direction, hop], device_id=target, device_id_type=MESH,
        )

    OFF = (0, -1, 1, 2)
    PASSED = ((), (0, 1, 2))

    def first_send(h, part):
        for direction in range(2):
            gcopy(h, part, 0, direction, 0, 0, 0, False, 1 - 2 * direction).start()
        gcopy(h, part, 0, 0, 1, 0, 0, False, 2).start()

    def first_wait(h, part, k):
        gcopy(h, part, 0, (0, 0, 1, 0)[k], k // 3, OFF[k], 0, False, 1).wait_recv()

    def second_send(h, part, k):
        for direction in range(2):
            gcopy(h, part, 1 + k, direction, 0, OFF[k], 0, False, 1 - 2 * direction).start()
        if k not in PASSED[h]:
            gcopy(h, part, 1 + k, 0, 1, OFF[k], 0, False, 2).start()

    def second_pass(h, part, k):
        for direction in range(2):
            step = 1 - 2 * direction
            gcopy(h, part, 1 + k, direction, 0, OFF[k], -step, False, step).wait_recv()
            gcopy(h, part, 1 + k, direction, 1, OFF[k], -step, True, step).start()

    def second_wait(h, part, k):
        if k in PASSED[h]:
            for direction in range(2):
                gcopy(h, part, 1 + k, direction, 1, OFF[k], 2, True, 1).wait_recv()
        else:
            for direction in range(2):
                step = 1 - 2 * direction
                gcopy(h, part, 1 + k, direction, 0, OFF[k], -step, False, step).wait_recv()
            gcopy(h, part, 1 + k, 0, 1, OFF[k], 2, False, 1).wait_recv()

    def gather0(h, part):
        first_send(h, part)
        second_send(h, part, 0)

    def gather1(h):
        for k in (1, 2, 3):
            for part in range(2):
                first_wait(h, part, k)
                second_send(h, part, k)
        if 0 in PASSED[h]:
            for part in range(2):
                second_pass(h, part, 0)

    def gather2(h):
        for k in PASSED[h]:
            if k > 0:
                for part in range(2):
                    second_pass(h, part, k)

    def pass_on(r, s):
        if s == 4:
            zcopy(0, r, zat(4), 3, True).wait_recv()
            zcopy(1, r, zat(4), 3, True).wait_recv()
            bcopy(r, zat(4), core).start()
            return
        for direction in range(2):
            owner = zat(-s if direction == 0 else s)
            zcopy(direction, r, owner, s - 1).wait_recv()
            zcopy(direction, r, owner, s, s == 3).start()
            bcopy(r, owner, core).start()

    def from_sibling(r, owner):
        bcopy(r, owner, 1 - core).wait_recv()

    def add(r, s, rounds=1):
        owners = {0: 1, 4: 1}.get(s, 2)

        def step(i, carry):
            at = r + i // owners
            owner = zat(s * (2 * (i % owners) - 1))
            from_sibling(at, owner)
            project(at, owner, first=s == 0)
            return carry

        lax.fori_loop(0, rounds * owners, step, 0)

    def finish_keys(g):
        add(3 * g, 4)
        kv[g, 0, 1] = normed(3 * g, kg[g:g + 1, :])
        send_halo(g, 0)
        add(3 * g + 1, 4)
        kv[g, 1, 1] = acc[3 * g + 1].astype(BF16)
        send_halo(g, 1)

    def finish_query(g):
        add(3 * g + 2, 4)
        qbuf[...] = normed(3 * g + 2, qg[g:g + 1, :])

    def mix(h, part, k):
        rows = pl.ds(part * 256, 256)
        owners = []
        for j in range(4):
            if part == 0:
                owners.append(j * NX + (x + OFF[k] + NX) % NX)
            else:
                owners.append((y + OFF[k] + NY) % NY * NX + j)
        left = jnp.concatenate([att[h, owner, rows, :] for owner in owners], axis=1)
        right = jnp.concatenate([wg[6 + h, owner] for owner in owners], axis=1)
        mixed = lax.dot_general(
            left, right, (((1,), (1,)), ((), ())), preferred_element_type=F32
        )
        if h == 0 and k == 0:
            oacc[rows, :] = mixed
        elif h == 1 and k == 3:
            out[rows, :] = (oacc[rows, :] + mixed).astype(BF16)
        else:
            oacc[rows, :] += mixed

    frames.wait()
    add(0, 0, 3)
    for g in range(2):
        k, v, q, before = 3 * g, 3 * g + 1, 3 * g + 2, 3 * g - 1
        pass_on(k, 1)
        pass_on(v, 1)
        if g == 1:
            send_own(q)
            pass_on(before, 4)
            add(k, 0, 3)
        add(k, 1, 2)
        if g == 1:
            finish_query(0)
            attend_near(0)
        pass_on(k, 2)
        pass_on(v, 2)
        if g == 1:
            attend_far(0, 0)
        pass_on(q, 1)
        if g == 1:
            attend_far(0, 1)
        add(k, 2, 2)
        add(q, 1)
        pass_on(k, 3)
        pass_on(v, 3)
        pass_on(q, 2)
        if g == 0:
            send_own(3)
            send_own(4)
        add(k, 3, 2)
        add(q, 2)
        if g == 1:
            gather1(0)
        pass_on(q, 3)
        pass_on(k, 4)
        pass_on(v, 4)
        finish_keys(g)
        if g == 1:
            send_own(6)
            send_own(7)
        add(q, 3)
    pass_on(5, 4)
    finish_query(1)
    attend_near(1)
    attend_far(1, 0)
    attend_far(1, 1)
    for s in range(1, 5):
        for r in (6, 7):
            pass_on(r, s)
        if s == 2:
            gather1(1)
        if s == 3:
            gather2(1)
    for r in (6, 7):
        for owner in range(NZ):
            from_sibling(r, owner)
    gather2(0)
    for h in range(2):
        for k in range(4):
            for part in range(2):
                second_wait(h, part, k)
                mix(h, part, k)

    for sent, sem in (
        (wg.at[pl.ds(0, 7), pl.ds(0, 8)], zsend),
        (wg.at[pl.ds(0, 4)], bsend),
        (kv.at[:, :, pl.ds(0, 2)], hsend),
        (att.at[:, pl.ds(0, 15)], gsend),
    ):
        pltpu.make_async_copy(sent, sent, sem).wait()


def body(frames, proj_weight, out_weight, query_gain, key_gain, key_tiles, key_counts):
    anywhere = pl.BlockSpec(memory_space=pl.ANY)
    vmem = pl.BlockSpec(memory_space=pltpu.VMEM)
    dma = pltpu.SemaphoreType.DMA
    return pl.pallas_call(
        kernel,
        out_shape=jax.ShapeDtypeStruct((TOK, ROWS), BF16),
        in_specs=[anywhere] * 3 + [vmem] * 4,
        out_specs=vmem,
        scratch_shapes=[
            pltpu.VMEM((8, NC, ROWS, HD), BF16),
            pltpu.VMEM((TOK, D), BF16),
            pltpu.VMEM((6, TOK, HD), F32),
            pltpu.VMEM((TOK, HD), BF16),
            pltpu.VMEM((2, 2, 3, TOK, HD), BF16),
            pltpu.VMEM((2, 16, TOK, HD), BF16),
            pltpu.VMEM((2, 3, QT, 1, TOK), F32),
            pltpu.VMEM((TOK, ROWS), F32),
            pltpu.VMEM((TOK, HD), F32),
            pltpu.VMEM((TOK, HD), F32),
            dma, dma((8,)),
            dma, dma((2, 8, 4)),
            dma, dma((8, 8)),
            dma, dma((2, 2, 2)),
            dma, dma((2, 2, 5, 2, 2)),
        ],
        compiler_params=pltpu.CompilerParams(
            collective_id=0, has_side_effects=True, vmem_limit_bytes=56 * 2**20
        ),
        cost_estimate=pl.CostEstimate(
            flops=8 * 10**9, bytes_accessed=8 * 10**6, transcendentals=2 * 10**6
        ),
        name="layer",
    )(
        frames, proj_weight, out_weight, query_gain.reshape(2, HD), key_gain.reshape(2, HD),
        key_tiles, key_counts,
    )


def solution(mesh):
    placed = (
        P("ctx", None),
        P(None, "ctx", "dp"),
        P("dp", "ctx"),
        P("dp"),
        P("dp"),
        P("dp", "ctx", None),
        P("dp", "ctx"),
    )
    return jax.shard_map(
        body, mesh=mesh, in_specs=placed, out_specs=P("ctx", "dp"), check_vma=False
    )
```

time: 104 us -> 92.3 us (0.89)
  Pallas kernels: 102 us -> 90.4 us
    pallas_call x1, Pallas kernels: 102 us -> 90.4 us  [body(): pl.pallas_call(kernel, out_shape=jax.ShapeDtypeStruct((TOK, ROWS), BF16),...]
where the time goes in v2:
time: 92.3 us; the launch traced here: 92.2 us
  Pallas kernels  90.4 us (98%)
  local copies, waits for them, and re-layouts  1.78 us (2%)
    pallas_call x1, Pallas kernels, body(): pl.pallas_call(kernel, out_shape=jax.ShapeDtypeStruct((TOK, ROWS), BF16),...  90.4 us

profile of v2, /device:TPU:1, one launch (start us, length us, event | category | flops | bytes accessed | tf_op | source)
XLA Modules:
  0.0 92.2 jit_solution(13385060820425440420)
XLA Ops:
  0.0 90.4 %layer.1 = bf16[512,384]{1,0:T(8,128)(2,1)} custom-call(bf16[512,6144]{1,0:T(8,128)(2,1)} %fr_hbm.1, bf16[3,384,256]{2,1,0:T(8,128)(2,1)} %pw_hbm.1, bf16[384,256]{1,0:T(8,128)(2,1)} %ow_hbm.1, f32[2,128]{1,0:T(2,128)} %bitcast.2, f32[2,128]{1,0:T(2,128)} %bitcast.3, s32[2,8,18]{2,1,0:T(8,128)} %kt.1, s32[2,8]{1,0:T(2,128)} %kc.1), custom_call_target="tpu_custom_call" | custom-call | flops 8000000000 | bytes 8000000 | tf_op jit(solution)/shard_map/layer/pallas_call | solution.py:374
  90.4 1.8 %copy.9 = bf16[512,384]{1,0:T(8,128)(2,1)} copy(bf16[512,384]{1,0:T(8,128)(2,1)} %layer.1) | data formatting | bytes 786432

commit v3 on v2

--- a/solution.py
+++ b/solution.py
@@ -60,12 +60,10 @@
         pl.semaphore_signal(barrier, inc=1, device_id=device, device_id_type=MESH)
     pl.semaphore_wait(barrier, len(greeted))
 
-    def zcopy(direction, r, owner, hop, half=False):
-        piece = wg.at[r, owner * 2 + core]
-        if half:
-            piece = piece.at[pl.ds(direction * HALF, HALF)]
+    def zcopy(direction, r, owner, hop, sub):
+        piece = wg.at[r, owner * 2 + core, pl.ds(sub * HALF, HALF)]
         return pltpu.make_async_remote_copy(
-            src_ref=piece, dst_ref=piece, send_sem=zsend, recv_sem=zrecv.at[direction, r, hop],
+            src_ref=piece, dst_ref=piece, send_sem=zsend, recv_sem=zrecv.at[direction, r, hop, sub],
             device_id=zdev(1 - 2 * direction), device_id_type=MESH,
         )
 
@@ -77,8 +75,9 @@
         )
 
     def send_own(r):
-        zcopy(0, r, z, 0).start()
-        zcopy(1, r, z, 0).start()
+        for i in range(2):
+            for direction in range(2):
+                zcopy(direction, r, z, 0, i ^ direction).start()
         bcopy(r, z, core).start()
 
     def zat(step):
@@ -238,15 +237,19 @@
 
     def pass_on(r, s):
         if s == 4:
-            zcopy(0, r, zat(4), 3, True).wait_recv()
-            zcopy(1, r, zat(4), 3, True).wait_recv()
+            for direction in range(2):
+                zcopy(direction, r, zat(4), 3, direction).wait_recv()
             bcopy(r, zat(4), core).start()
             return
-        for direction in range(2):
-            owner = zat(-s if direction == 0 else s)
-            zcopy(direction, r, owner, s - 1).wait_recv()
-            zcopy(direction, r, owner, s, s == 3).start()
-            bcopy(r, owner, core).start()
+        for i in range(2):
+            for direction in range(2):
+                sub = i ^ direction
+                owner = zat(-s if direction == 0 else s)
+                zcopy(direction, r, owner, s - 1, sub).wait_recv()
+                if s < 3 or sub == direction:
+                    zcopy(direction, r, owner, s, sub).start()
+        for step in (-s, s):
+            bcopy(r, zat(step), core).start()
 
     def from_sibling(r, owner):
         bcopy(r, owner, 1 - core).wait_recv()
@@ -275,7 +278,22 @@
         add(3 * g + 2, 4)
         qbuf[...] = normed(3 * g + 2, qg[g:g + 1, :])
 
-    def mix(h, part, k):
+    def mix_hop(s):
+        owners = []
+        for step in (s,) if s in (0, 4) else (-s, s):
+            from_sibling(6, zat(step))
+            owners += [zat(step) * 2, zat(step) * 2 + 1]
+        left = jnp.concatenate([att[0, owner] for owner in owners], axis=1)
+        right = jnp.concatenate([wg[6, owner] for owner in owners], axis=1)
+        mixed = lax.dot_general(
+            left, right, (((1,), (1,)), ((), ())), preferred_element_type=F32
+        )
+        if s == 0:
+            oacc[...] = mixed
+        else:
+            oacc[...] += mixed
+
+    def mix(part, k):
         rows = pl.ds(part * 256, 256)
         owners = []
         for j in range(4):
@@ -283,17 +301,19 @@
                 owners.append(j * NX + (x + OFF[k] + NX) % NX)
             else:
                 owners.append((y + OFF[k] + NY) % NY * NX + j)
-        left = jnp.concatenate([att[h, owner, rows, :] for owner in owners], axis=1)
-        right = jnp.concatenate([wg[6 + h, owner] for owner in owners], axis=1)
-        mixed = lax.dot_general(
+        left = jnp.concatenate([att[1, owner, rows, :] for owner in owners], axis=1)
+        right = jnp.concatenate([wg[7, owner] for owner in owners], axis=1)
+        mixed = oacc[rows, :] + lax.dot_general(
             left, right, (((1,), (1,)), ((), ())), preferred_element_type=F32
         )
-        if h == 0 and k == 0:
+        if k == 3:
+            out[rows, :] = mixed.astype(BF16)
+        else:
             oacc[rows, :] = mixed
-        elif h == 1 and k == 3:
-            out[rows, :] = (oacc[rows, :] + mixed).astype(BF16)
-        else:
-            oacc[rows, :] += mixed
+
+    def pass_all(*steps):
+        for r, s in steps:
+            pass_on(r, s)
 
     frames.wait()
     add(0, 0, 3)
@@ -331,9 +351,10 @@
         pass_on(q, 3)
         pass_on(k, 4)
         pass_on(v, 4)
+        if g == 1:
+            send_own(6)
         finish_keys(g)
         if g == 1:
-            send_own(6)
             send_own(7)
         add(q, 3)
     pass_on(5, 4)
@@ -341,22 +362,23 @@
     attend_near(1)
     attend_far(1, 0)
     attend_far(1, 1)
-    for s in range(1, 5):
-        for r in (6, 7):
-            pass_on(r, s)
-        if s == 2:
-            gather1(1)
-        if s == 3:
-            gather2(1)
-    for r in (6, 7):
-        for owner in range(NZ):
-            from_sibling(r, owner)
-    gather2(0)
-    for h in range(2):
-        for k in range(4):
-            for part in range(2):
-                second_wait(h, part, k)
-                mix(h, part, k)
+    pass_all((6, 1), (7, 1), (6, 2), (7, 2))
+    gather1(1)
+    pass_all((6, 3), (7, 3))
+    for k in range(4):
+        for part in range(2):
+            second_wait(0, part, k)
+    for s in range(4):
+        mix_hop(s)
+    pass_all((6, 4), (7, 4))
+    gather2(1)
+    mix_hop(4)
+    for owner in range(NZ):
+        from_sibling(7, owner)
+    for k in range(4):
+        for part in range(2):
+            second_wait(1, part, k)
+            mix(part, k)
 
     for sent, sem in (
         (wg.at[pl.ds(0, 7), pl.ds(0, 8)], zsend),
@@ -388,7 +410,7 @@
             pltpu.VMEM((TOK, HD), F32),
             pltpu.VMEM((TOK, HD), F32),
             dma, dma((8,)),
-            dma, dma((2, 8, 4)),
+            dma, dma((2, 8, 4, 2)),
             dma, dma((8, 8)),
             dma, dma((2, 2, 2)),
             dma, dma((2, 2, 5, 2, 2)),

time: 92.3 us -> 91 us (0.986)
  Pallas kernels: 90.4 us -> 89.1 us
    pallas_call x1, Pallas kernels: 90.4 us -> 89.1 us  [body(): pl.pallas_call(kernel, out_shape=jax.ShapeDtypeStruct((TOK, ROWS), BF16),...]
where the time goes in v3:
time: 91 us; the launch traced here: 90.8 us
  Pallas kernels  89.1 us (98%)
  local copies, waits for them, and re-layouts  1.78 us (2%)
    pallas_call x1, Pallas kernels, body(): pl.pallas_call(kernel, out_shape=jax.ShapeDtypeStruct((TOK, ROWS), BF16),...  89.1 us

profile of v3, /device:TPU:1, one launch (start us, length us, event | category | flops | bytes accessed | tf_op | source)
XLA Modules:
  0.0 90.8 jit_solution(5649375184995340763)
XLA Ops:
  0.0 89.1 %layer.1 = bf16[512,384]{1,0:T(8,128)(2,1)} custom-call(bf16[512,6144]{1,0:T(8,128)(2,1)} %fr_hbm.1, bf16[3,384,256]{2,1,0:T(8,128)(2,1)} %pw_hbm.1, bf16[384,256]{1,0:T(8,128)(2,1)} %ow_hbm.1, f32[2,128]{1,0:T(2,128)} %bitcast.2, f32[2,128]{1,0:T(2,128)} %bitcast.3, s32[2,8,18]{2,1,0:T(8,128)} %kt.1, s32[2,8]{1,0:T(2,128)} %kc.1), custom_call_target="tpu_custom_call" | custom-call | flops 8000000000 | bytes 8000000 | tf_op jit(solution)/shard_map/layer/pallas_call | solution.py:396
  89.1 1.8 %copy.9 = bf16[512,384]{1,0:T(8,128)(2,1)} copy(bf16[512,384]{1,0:T(8,128)(2,1)} %layer.1) | data formatting | bytes 786432

commit v4 on v3

--- a/solution.py
+++ b/solution.py
@@ -218,7 +218,9 @@
 
     def gather0(h, part):
         first_send(h, part)
-        second_send(h, part, 0)
+        if part == 1:
+            second_send(h, 0, 0)
+            second_send(h, 1, 0)
 
     def gather1(h):
         for k in (1, 2, 3):

time: 91 us -> 91 us (level)
  no operation moved by 1% of the time
where the time goes in v4:
time: 91 us; the launch traced here: 90.8 us
  Pallas kernels  89 us (98%)
  local copies, waits for them, and re-layouts  1.78 us (2%)
    pallas_call x1, Pallas kernels, body(): pl.pallas_call(kernel, out_shape=jax.ShapeDtypeStruct((TOK, ROWS), BF16),...  89 us

profile of v4, /device:TPU:1, one launch (start us, length us, event | category | flops | bytes accessed | tf_op | source)
XLA Modules:
  0.0 90.8 jit_solution(17643989311758166289)
XLA Ops:
  0.0 89.0 %layer.1 = bf16[512,384]{1,0:T(8,128)(2,1)} custom-call(bf16[512,6144]{1,0:T(8,128)(2,1)} %fr_hbm.1, bf16[3,384,256]{2,1,0:T(8,128)(2,1)} %pw_hbm.1, bf16[384,256]{1,0:T(8,128)(2,1)} %ow_hbm.1, f32[2,128]{1,0:T(2,128)} %bitcast.2, f32[2,128]{1,0:T(2,128)} %bitcast.3, s32[2,8,18]{2,1,0:T(8,128)} %kt.1, s32[2,8]{1,0:T(2,128)} %kc.1), custom_call_target="tpu_custom_call" | custom-call | flops 8000000000 | bytes 8000000 | tf_op jit(solution)/shard_map/layer/pallas_call | solution.py:398
  89.0 1.8 %copy.9 = bf16[512,384]{1,0:T(8,128)(2,1)} copy(bf16[512,384]{1,0:T(8,128)(2,1)} %layer.1) | data formatting | bytes 786432
